TPU v7x, 32 devices: a whole 2x2x4 slice. The times are simulated.
32 devices in a mesh: dp: 8 (over z, x), fsdp: 4 (over y, core).
Axes of the slice: x: 2, y: 2, z: 4, core: 2. Of those that a mesh axis runs over, the one named last changes fastest.
Arguments:
- img_feat: bfloat16 [1536, 1536], P(('dp', 'fsdp')), may hold values from -6 to 6
- txt_feat: bfloat16 [1536, 1536], P(('dp', 'fsdp')), may hold values from -6 to 6
- img_weight: bfloat16 [1536, 1536], P('fsdp'), may hold values from -0.15625 to 0.15625
- txt_weight: bfloat16 [1536, 1536], P('fsdp'), may hold values from -0.15625 to 0.15625
- log_temp: float32 [1], replicated, may hold values from 1.5 to 2.5
- bias: float32 [1], replicated, may hold values from -6 to -4
Outputs:
- grad_img_weight: float32 [1536, 1536], P('fsdp')
- grad_txt_weight: float32 [1536, 1536], P('fsdp')
All inputs are finite; a program needn't handle non-finite values.
Results may differ from a plain program's by a relative error of at most 0.0053.
Values may be sent and summed in bfloat16 or wider, within the bound.
A program may use at most 64 MiB of HBM per device.

v0:
```python
import jax
import jax.numpy as jnp
from jax import lax
from jax.sharding import PartitionSpec as P

EPS = 1e-06


def factor(y_rows):
    mean_sq = jnp.mean(y_rows * y_rows, -1, keepdims=True)
    return (lax.rsqrt(mean_sq + EPS) * y_rows.shape[-1] ** (-0.5), mean_sq)


def back_norm(y_rows, grad_rows):
    norm_factor, mean_sq = factor(y_rows)
    inner_sum = jnp.sum(y_rows * grad_rows, -1, keepdims=True)
    result = norm_factor * grad_rows - norm_factor * y_rows * inner_sum / (
        y_rows.shape[-1] * (mean_sq + EPS)
    )
    return result.astype(jnp.bfloat16)


def on_device(img_feat, txt_feat, img_weight, txt_weight, log_temp, bias):
    row_count = img_feat.shape[0]
    groups = lax.axis_size("fsdp")
    dp_index = lax.axis_index("dp")
    fsdp_index = lax.axis_index("fsdp")
    img_cols, txt_cols = (
        lax.all_to_all(img_feat, "fsdp", split_axis=1, concat_axis=0, tiled=True),
        lax.all_to_all(txt_feat, "fsdp", split_axis=1, concat_axis=0, tiled=True),
    )
    y_img = jnp.dot(
        img_feat,
        lax.all_gather(img_weight, "fsdp", axis=0, tiled=True),
        preferred_element_type=jnp.float32,
    )
    y_txt = jnp.dot(
        txt_feat,
        lax.all_gather(txt_weight, "fsdp", axis=0, tiled=True),
        preferred_element_type=jnp.float32,
    )
    img_factor, unused_img = factor(y_img)
    z_own = (y_img * img_factor).astype(jnp.bfloat16)
    image_block = lax.all_gather(z_own, "fsdp", axis=0, tiled=True)
    txt_factor, unused_txt = factor(y_txt)
    z_txt = (y_txt * txt_factor).astype(jnp.bfloat16)
    temp_scale = jnp.exp(log_temp[0])
    bias_value = bias[0]
    group_rows = image_block.shape[0]
    image_ids = dp_index * groups * row_count + jnp.arange(group_rows, dtype=jnp.int32)
    text_piece = lax.all_gather(z_txt, "dp", axis=0, tiled=True)
    length = text_piece.shape[0]
    text_pos = jnp.arange(length, dtype=jnp.int32)
    text_ids = (text_pos // row_count * groups + fsdp_index) * row_count + text_pos % row_count
    logits = (
        temp_scale
        * lax.dot_general(
            image_block, text_piece, (((1,), (1,)), ((), ())), preferred_element_type=jnp.float32
        )
        + bias_value
    )
    pair_label = jnp.where(image_ids[:, None] == text_ids[None, :], 1.0, -1.0).astype(jnp.float32)
    pair_weight = (temp_scale * (-pair_label * jax.nn.sigmoid(-pair_label * logits))).astype(
        jnp.bfloat16
    )
    grad_sum = jnp.dot(pair_weight, text_piece, preferred_element_type=jnp.float32)
    grad_txt = lax.psum_scatter(
        lax.dot_general(
            pair_weight, image_block, (((0,), (0,)), ((), ())), preferred_element_type=jnp.float32
        ),
        "dp",
        scatter_dimension=0,
        tiled=True,
    )
    grad_img = lax.psum_scatter(grad_sum, "fsdp", scatter_dimension=0, tiled=True)
    dy_img = back_norm(y_img, grad_img)
    dy_txt = back_norm(y_txt, grad_txt)
    dy_img_group, dy_txt_group = (
        lax.all_gather(dy_img, "fsdp", axis=0, tiled=True),
        lax.all_gather(dy_txt, "fsdp", axis=0, tiled=True),
    )
    weight_img = lax.dot_general(
        img_cols, dy_img_group, (((0,), (0,)), ((), ())), preferred_element_type=jnp.float32
    )
    weight_txt = lax.dot_general(
        txt_cols, dy_txt_group, (((0,), (0,)), ((), ())), preferred_element_type=jnp.float32
    )
    grad_img_weight, grad_txt_weight = lax.psum((weight_img, weight_txt), "dp")
    return (grad_img_weight, grad_txt_weight)


def solution(mesh):
    placed = (
        P(("dp", "fsdp"), None),
        P(("dp", "fsdp"), None),
        P("fsdp", None),
        P("fsdp", None),
        P(),
        P(),
    )
    return jax.shard_map(
        on_device,
        mesh=mesh,
        in_specs=placed,
        out_specs=(P("fsdp", None), P("fsdp", None)),
        check_vma=False,
    )
```

profile of v0, /device:TPU:0, one launch (start us, length us, event | category | flops | bytes accessed | tf_op | source)
XLA Modules:
  0.0 426.2 jit_solution(16601721012214406229)
XLA Ops:
  7.2 0.7 all-gather.6.cloned.1.call-update
  8.0 0.7 all-gather.4.cloned.1.call-update
  8.7 41.0 %all-gather.6.cloned.1.call-done = bf16[1536,1536]{1,0:T(8,128)(2,1)} async-done(((bf16[384,1536]{1,0:T(8,128)(2,1)}), bf16[1536,1536]{1,0:T(8,128)(2,1)}) %all-gather.6.cloned.1.call-update) | async-done | bytes 4718608 | tf_op jit(solution)/shard_map/all_gather | solution.py:39
  49.8 3.4 multiply_reduce_fusion.2
  53.1 0.8 multiply_convert_fusion
  53.9 0.0 reduce-scatter.3.cloned.1.call-start
  55.3 33.5 %all-gather.4.cloned.1.call-done = bf16[1536,1536]{1,0:T(8,128)(2,1)} async-done(((bf16[384,1536]{1,0:T(8,128)(2,1)}), bf16[1536,1536]{1,0:T(8,128)(2,1)}) %all-gather.4.cloned.1.call-update) | async-done | bytes 4718608 | tf_op jit(solution)/shard_map/all_gather | solution.py:34
  88.8 3.4 multiply_reduce_fusion.3
  92.2 0.1 multiply_convert_fusion.1
  92.3 7.6 %all_gather.19 = bf16[192,1536]{1,0:T(8,128)(2,1)S(1)} all-gather(bf16[48,1536]{1,0:T(8,128)(2,1)S(1)} %multiply_convert_fusion.1), channel_id=1, replica_groups=mesh['dp'=8,'fsdp'=4] {'fsdp'}, dimensions={0}, use_global_device_ids=true | all-gather | bytes 737280 | tf_op jit(solution)/shard_map/all_gather | solution.py:44
  99.8 32.8 %all-gather.8.cloned.1.call-done = bf16[384,1536]{1,0:T(8,128)(2,1)} async-done(((bf16[48,1536]{1,0:T(8,128)(2,1)}), bf16[384,1536]{1,0:T(8,128)(2,1)}) %all-gather.8.cloned.1.call-update) | async-done | bytes 1179664 | tf_op jit(solution)/shard_map/all_gather | solution.py:51
  132.7 2.0 fusion.8
  134.7 1.5 fusion.20
  136.2 1.9 fusion.21
  138.1 0.7 copy.25
  138.8 3.3 all-to-all-start
  142.2 0.7 copy.24
  142.8 18.0 %reduce-scatter.3.cloned.1.call-done = f32[48,1536]{1,0:T(8,128)} async-done(((f32[192,1536]{1,0:T(8,128)}), f32[48,1536]{1,0:T(8,128)}) %reduce-scatter.3.cloned.1.call-update) | async-done | bytes 294928 | tf_op jit(solution)/shard_map/reduce_scatter | solution.py:75
  160.8 1.1 multiply_reduce_fusion.1
  161.9 1.1 subtract_convert_fusion.1
  163.0 7.1 %all_gather.22 = bf16[192,1536]{1,0:T(8,128)(2,1)S(1)} all-gather(bf16[48,1536]{1,0:T(8,128)(2,1)S(1)} %subtract_convert_fusion.1), channel_id=1, replica_groups=mesh['dp'=8,'fsdp'=4] {'fsdp'}, dimensions={0}, use_global_device_ids=true | all-gather | bytes 737280 | tf_op jit(solution)/shard_map/all_gather | solution.py:79
  170.1 3.3 all-to-all-start.1
  173.5 0.0 all-reduce.3.cloned.1.call-start
  173.5 2.0 convolution_bitcast_fusion.1
  175.6 58.5 %reduce-scatter.5.cloned.1.call-done = f32[48,1536]{1,0:T(8,128)} async-done(((f32[384,1536]{1,0:T(8,128)}), f32[48,1536]{1,0:T(8,128)}) %reduce-scatter.5.cloned.1.call-update) | async-done | bytes 294928 | tf_op jit(solution)/shard_map/reduce_scatter | solution.py:67
  234.0 1.1 multiply_reduce_fusion
  235.1 1.1 subtract_convert_fusion
  236.2 7.5 %all_gather.23 = bf16[192,1536]{1,0:T(8,128)(2,1)S(1)} all-gather(bf16[48,1536]{1,0:T(8,128)(2,1)S(1)} %subtract_convert_fusion), channel_id=1, replica_groups=mesh['dp'=8,'fsdp'=4] {'fsdp'}, dimensions={0}, use_global_device_ids=true | all-gather | bytes 737280 | tf_op jit(solution)/shard_map/all_gather | solution.py:80
  243.8 2.0 convolution_bitcast_fusion
  245.8 168.4 %all-reduce.3.cloned.1.call-done = (f32[384,1536]{0,1:T(8,128)}, f32[384,1536]{0,1:T(8,128)}) async-done(((f32[384,1536]{0,1:T(8,128)}, f32[384,1536]{0,1:T(8,128)}), (f32[384,1536]{0,1:T(8,128)}, f32[384,1536]{0,1:T(8,128)})) %all-reduce.3.cloned.1.call-update) | async-done | bytes 4718608 | tf_op jit(solution)/shard_map/psum | solution.py:88
  414.2 3.2 copy.18
  417.4 1.9 copy.19
  (22 shorter events, 0.3 us)
Async XLA Ops:
  7.2 42.6 %copy-start.3 = (bf16[48,1536]{1,0:T(8,128)(2,1)S(1)}, bf16[48,1536]{1,0:T(8,128)(2,1)}, u32[]{:S(2)}) copy-start(bf16[48,1536]{1,0:T(8,128)(2,1)} %param.7) | copy-start | bytes 442372
  7.2 42.6 %all-gather.6.cloned.1.call-start = ((), (), s32[]{:S(2)}) async-start(), calls=%async_computation.5 | async-start | bytes 5898240 | tf_op jit(solution)/shard_map/all_gather | solution.py:39
  7.9 80.9 %all-gather.4.cloned.1.call-start = ((), (), s32[]{:S(2)}) async-start(), calls=%async_computation.4 | async-start | bytes 5898240 | tf_op jit(solution)/shard_map/all_gather | solution.py:34
  8.7 80.2 %copy-start.2 = (bf16[48,1536]{1,0:T(8,128)(2,1)S(1)}, bf16[48,1536]{1,0:T(8,128)(2,1)}, u32[]{:S(2)}) copy-start(bf16[48,1536]{1,0:T(8,128)(2,1)} %param.6) | copy-start | bytes 442372
  8.7 124.0 %all-gather.8.cloned.1.call-start = ((), (), s32[]{:S(2)}) async-start(), calls=%async_computation.6 | async-start | bytes 1327104 | tf_op jit(solution)/shard_map/all_gather | solution.py:51
  53.9 106.9 %reduce-scatter.3.cloned.1.call-start = ((), (), s32[]{:S(2)}) async-start(), calls=%async_computation.7 | async-start | bytes 1474560 | tf_op jit(solution)/shard_map/reduce_scatter | solution.py:75
  132.7 2.0 copy-start.1
  136.2 97.9 %reduce-scatter.5.cloned.1.call-start = ((), (), s32[]{:S(2)}) async-start(), calls=%async_computation.8 | async-start | bytes 2654208 | tf_op jit(solution)/shard_map/reduce_scatter | solution.py:67
  138.8 31.3 %all-to-all-start = ((bf16[48,4,384]{2,0,1:T(8,128)(2,1)}), bf16[48,4,384]{2,0,1:T(8,128)(2,1)S(1)}, u32[]{:S(2)}, u32[]{:S(2)}) async-start(bf16[48,4,384]{2,0,1:T(8,128)(2,1)} %bitcast.33), calls=%async_computation.1 | async-start | bytes 294912 | tf_op jit(solution)/shard_map/all_to_all | solution.py:29
  170.1 73.6 %all-to-all-start.1 = ((bf16[48,4,384]{2,0,1:T(8,128)(2,1)}), bf16[48,4,384]{2,0,1:T(8,128)(2,1)S(1)}, u32[]{:S(2)}, u32[]{:S(2)}) async-start(bf16[48,4,384]{2,0,1:T(8,128)(2,1)} %bitcast.32), calls=%async_computation.3 | async-start | bytes 294912 | tf_op jit(solution)/shard_map/all_to_all | solution.py:30
  173.5 240.7 %all-reduce.3.cloned.1.call-start = ((), (), s32[]{:S(2)}) async-start(), calls=%async_computation.9 | async-start | bytes 9437184 | tf_op jit(solution)/shard_map/psum | solution.py:88
  414.2 3.2 copy-start
Sparse Core Ops, SparseCore 0:
  9.6 40.1 all-gather.5
  51.3 37.4 all-gather.3
  91.6 41.0 all-gather.7
  136.3 24.4 reduce-scatter.2
  165.1 68.8 reduce-scatter.4
  245.9 168.2 all-reduce.2
where the time goes:
time: 427 us; the launch traced here: 426 us
  waiting for transfers between devices  354 us (83%)
  blocking collectives  22.2 us (5%)
  matrix products  16.1 us (4%)
  between operations  15.6 us (4%)
  starting transfers between devices  6.91 us (2%)
  local copies, waits for them, and re-layouts  6.51 us (2%)
  other arithmetic  5.27 us (1%)
    psum x1, waiting for transfers between devices, on_device(): grad_img_weight, grad_txt_weight = lax.psum((weight_img, weight_txt), 'dp')  168 us
    reduce_scatter x1, waiting for transfers between devices, on_device(): lax.psum_scatter(lax.dot_general(pair_weight, image_block, (((0,), (0,)),...  58.5 us
    all_gather x1, waiting for transfers between devices, on_device(): lax.all_gather(txt_weight, 'fsdp', axis=0, tiled=True)  41 us
    all_gather x1, waiting for transfers between devices, on_device(): lax.all_gather(img_weight, 'fsdp', axis=0, tiled=True)  33.5 us
    all_gather x1, waiting for transfers between devices, on_device(): text_piece = lax.all_gather(z_txt, 'dp', axis=0, tiled=True)  32.8 us
    reduce_scatter x1, waiting for transfers between devices, on_device(): lax.psum_scatter(grad_sum, 'fsdp', scatter_dimension=0, tiled=True)  18 us
  transfers between devices with their start and end apart: 8, of which 6 were waited for; matrix products, arithmetic and copies ran while one was open for 4% of the time, Pallas kernels for 0%

commit v1 on v0

--- a/solution.py
+++ b/solution.py
@@ -1,6 +1,10 @@
+import functools
+
 import jax
 import jax.numpy as jnp
 from jax import lax
+from jax.experimental import pallas as pl
+from jax.experimental.pallas import tpu as pltpu
 from jax.sharding import PartitionSpec as P
 
 EPS = 1e-06
@@ -20,7 +24,7 @@
     return result.astype(jnp.bfloat16)
 
 
-def on_device(img_feat, txt_feat, img_weight, txt_weight, log_temp, bias):
+def by_collectives(img_feat, txt_feat, img_weight, txt_weight, log_temp, bias):
     row_count = img_feat.shape[0]
     groups = lax.axis_size("fsdp")
     dp_index = lax.axis_index("dp")
@@ -89,6 +93,273 @@
     return (grad_img_weight, grad_txt_weight)
 
 
+BF16 = jnp.bfloat16
+F32 = jnp.float32
+SIDE = 2
+
+
+def dot(a, b, a_dim, b_dim):
+    return lax.dot_general(a, b, (((a_dim,), (b_dim,)), ((), ())), preferred_element_type=F32)
+
+
+def kernel(
+    dims, img, txt, w_img, w_txt, log_temp, bias, out,
+    cols, feats, part, part16, part_in, y_keep, z_img, z_txt,
+    d_img, d_img16, d_img_in, d_txt, d_txt16, d_txt_in, dy, dy_all,
+    send_sem, recv_sem,
+):
+    dp_n, groups, rows, width, embed = dims
+    depth_n = dp_n // SIDE
+    plane_n = SIDE * groups
+    wide, tall = width // groups, embed // depth_n
+    me_dp, me_f = lax.axis_index("dp"), lax.axis_index("fsdp")
+    depth, side = me_dp // SIDE, me_dp % SIDE
+    spot = side * groups + me_f
+    count = [0]
+
+    def send(source, target, to_dp, to_f):
+        number = count[0]
+        count[0] += 1
+        copy = pltpu.make_async_remote_copy(
+            src_ref=source, dst_ref=target,
+            send_sem=send_sem.at[number], recv_sem=recv_sem.at[number],
+            device_id=(to_dp, to_f), device_id_type=pl.DeviceIdType.MESH,
+        )
+        copy.start()
+        sent.append(copy)
+        return copy
+
+    sent = []
+
+    def at_spot(k):
+        other = (spot + k) % plane_n
+        return depth * SIDE + other // groups, other % groups
+
+    def at_depth(k):
+        return (depth + k) % depth_n
+
+    def lanes(start, size):
+        return pl.ds(pl.multiple_of(start * size, size), size)
+
+    barrier = pltpu.get_barrier_semaphore()
+    peers = [at_spot(k) for k in range(1, plane_n)]
+    peers += [
+        (at_depth(k) * SIDE + s, me_f) for k in range(1, depth_n) for s in range(SIDE)
+    ]
+    for peer in peers:
+        pl.semaphore_signal(barrier, inc=1, device_id=peer, device_id_type=pl.DeviceIdType.MESH)
+    pl.semaphore_wait(barrier, len(peers))
+
+    got_cols = []
+    for tower, feat in ((1, txt), (0, img)):
+        for k in range(1, groups):
+            to_f = (me_f + k) % groups
+            got_cols.append(
+                send(feat.at[:, lanes(to_f, wide)], cols.at[tower, me_f], me_dp, to_f)
+            )
+    for tower, feat in ((1, txt), (0, img)):
+        cols[tower, me_f] = feat[:, lanes(me_f, wide)]
+
+    tile = 384 if embed % 384 == 0 else 128
+    got_part = {}
+    for tower, weight in ((1, w_txt), (0, w_img)):
+        for k in range(1, groups):
+            got_cols.pop(0).wait_recv()
+
+        def y_tile(j, carry, tower=tower, weight=weight):
+            where = lanes(j, tile)
+            term = dot(cols[tower].reshape(groups * rows, wide), weight[:, where], 1, 0)
+            term = term.reshape(groups, rows, tile)
+            part[tower, :, :, where] = term
+            part16[tower, :, :, where] = term.astype(BF16)
+            return carry
+
+        lax.fori_loop(0, embed // tile, y_tile, 0)
+        got_part[tower] = [
+            send(part16.at[tower, (me_f + k) % groups], part_in.at[tower, k - 1],
+                 me_dp, (me_f + k) % groups)
+            for k in range(1, groups)
+        ]
+
+    feats[me_dp] = cols[side]
+    got_feats = []
+    for k in range(1, dp_n):
+        to_dp = (me_dp + k) % dp_n
+        got_feats.append(send(cols.at[to_dp % SIDE], feats.at[me_dp], to_dp, me_f))
+
+    def y_rows(tower):
+        for copy in got_part[tower]:
+            copy.wait_recv()
+        total = part[tower, me_f]
+        for k in range(1, groups):
+            total = total + part_in[tower, k - 1].astype(F32)
+        y_keep[tower] = total
+        norm_factor, _ = factor(total)
+        return (total * norm_factor).astype(BF16)
+
+    z_txt[depth] = y_rows(1)
+    got_txt = [
+        send(z_txt.at[depth], z_txt.at[depth], at_depth(k) * SIDE + side, me_f)
+        for k in range(1, depth_n)
+    ]
+    z_img[spot] = y_rows(0)
+    got_img = [
+        send(z_img.at[spot], z_img.at[spot], *at_spot(k)) for k in range(1, plane_n)
+    ]
+    for copy in got_txt + got_img:
+        copy.wait_recv()
+
+    n_img, n_txt = plane_n * rows, depth_n * rows
+    scale = jnp.exp(jnp.full((1, n_txt), log_temp[0], F32))
+    scores = dot(
+        z_img[...].reshape(n_img, embed), z_txt[...].reshape(n_txt, embed), 1, 1
+    )
+    scores = scale * scores + bias[0]
+    row = lax.broadcasted_iota(jnp.int32, (n_img, n_txt), 0) - spot * rows
+    col = lax.broadcasted_iota(jnp.int32, (n_img, n_txt), 1) - depth * rows
+    label = jnp.where((row == col) & (row >= 0) & (row < rows), 1.0, -1.0).astype(F32)
+    pair = (scale * (-label * jax.nn.sigmoid(-label * scores))).astype(BF16)
+
+    def txt_tile(j, carry):
+        where = lanes(j, tile)
+        term = dot(pair, z_img[:, :, where].reshape(n_img, tile), 0, 0)
+        term = term.reshape(depth_n, rows, tile)
+        d_txt[:, :, where] = term
+        d_txt16[:, :, where] = term.astype(BF16)
+        return carry
+
+    lax.fori_loop(0, embed // tile, txt_tile, 0)
+    got_txt = [
+        send(d_txt16.at[at_depth(k)], d_txt_in.at[k - 1], at_depth(k) * SIDE + side, me_f)
+        for k in range(1, depth_n)
+    ]
+
+    def img_tile(j, carry):
+        where = lanes(j, tile)
+        term = dot(pair, z_txt[:, :, where].reshape(n_txt, tile), 1, 0)
+        term = term.reshape(plane_n, rows, tile)
+        d_img[:, :, where] = term
+        d_img16[:, :, where] = term.astype(BF16)
+        return carry
+
+    lax.fori_loop(0, embed // tile, img_tile, 0)
+    got_img = [
+        send(d_img16.at[(spot + k) % plane_n], d_img_in.at[k - 1], *at_spot(k))
+        for k in range(1, plane_n)
+    ]
+
+    for tower, copies, own, arrived in (
+        (1, got_txt, d_txt[depth], d_txt_in),
+        (0, got_img, d_img[spot], d_img_in),
+    ):
+        for k, copy in enumerate(copies):
+            copy.wait_recv()
+            own = own + arrived[k].astype(F32)
+        dy[tower] = back_norm(y_keep[tower], own)
+
+    got_dy = []
+    for k in range(1, dp_n):
+        to_dp = (me_dp + k) % dp_n
+        got_dy.append(
+            send(dy.at[to_dp % SIDE, :, lanes(to_dp // SIDE, tall)], dy_all.at[me_f, me_dp],
+                 to_dp, me_f)
+        )
+    dy_all[me_f, me_dp] = dy[side, :, lanes(depth, tall)]
+    for copy in got_dy + got_feats:
+        copy.wait_recv()
+    half = groups // 2
+    across = (me_f + half) % groups
+    twin = me_f + 1 - 2 * (me_f % 2)
+    from_across = send(dy_all.at[me_f], dy_all.at[me_f], me_dp, across)
+    from_twin = send(dy_all.at[me_f], dy_all.at[me_f], me_dp, twin)
+
+    def grad_of(group):
+        left = feats[:, group].reshape(dp_n * rows, wide)
+        return dot(left, dy_all[group].reshape(dp_n * rows, tall), 0, 0)
+
+    grad = grad_of(me_f)
+    from_twin.wait_recv()
+    grad = grad + grad_of(twin)
+    from_across.wait_recv()
+    passed_on = send(dy_all.at[across], dy_all.at[across], me_dp, twin)
+    grad = grad + grad_of(across)
+    passed_on.wait_recv()
+    grad = grad + grad_of((twin + half) % groups)
+    out[side, depth] = grad.astype(BF16)
+
+    beside = depth * SIDE + (1 - side)
+    along = [
+        send(out.at[side, depth], out.at[side, depth], at_depth(k) * SIDE + side, me_f)
+        for k in range(1, depth_n)
+    ]
+    over = [send(out.at[side, depth], out.at[side, depth], beside, me_f)]
+    for k in range(1, depth_n):
+        along[k - 1].wait_recv()
+        place = (depth + depth_n - k) % depth_n
+        over.append(send(out.at[side, place], out.at[side, place], beside, me_f))
+    for copy in over:
+        copy.wait_recv()
+    for copy in sent:
+        copy.wait_send()
+
+
+def in_one_kernel(dp_n, groups, img_feat, txt_feat, img_weight, txt_weight, log_temp, bias):
+    rows, width = img_feat.shape
+    wide, embed = img_weight.shape
+    depth_n, plane_n = dp_n // SIDE, SIDE * groups
+    tall = embed // depth_n
+    copies = 2 * 2 * (groups - 1) + 2 * (dp_n - 1) + 3 + 2 * (depth_n - 1 + plane_n - 1)
+    copies += 2 * depth_n - 1
+    vmem = pl.BlockSpec(memory_space=pltpu.VMEM)
+    smem = pl.BlockSpec(memory_space=pltpu.SMEM)
+    tiles = pl.pallas_call(
+        functools.partial(kernel, (dp_n, groups, rows, width, embed)),
+        out_shape=jax.ShapeDtypeStruct((SIDE, depth_n, wide, tall), BF16),
+        in_specs=[vmem] * 4 + [smem] * 2,
+        out_specs=vmem,
+        scratch_shapes=[
+            pltpu.VMEM((2, groups, rows, wide), BF16),
+            pltpu.VMEM((dp_n, groups, rows, wide), BF16),
+            pltpu.VMEM((2, groups, rows, embed), F32),
+            pltpu.VMEM((2, groups, rows, embed), BF16),
+            pltpu.VMEM((2, groups - 1, rows, embed), BF16),
+            pltpu.VMEM((2, rows, embed), F32),
+            pltpu.VMEM((plane_n, rows, embed), BF16),
+            pltpu.VMEM((depth_n, rows, embed), BF16),
+            pltpu.VMEM((plane_n, rows, embed), F32),
+            pltpu.VMEM((plane_n, rows, embed), BF16),
+            pltpu.VMEM((plane_n - 1, rows, embed), BF16),
+            pltpu.VMEM((depth_n, rows, embed), F32),
+            pltpu.VMEM((depth_n, rows, embed), BF16),
+            pltpu.VMEM((depth_n - 1, rows, embed), BF16),
+            pltpu.VMEM((2, rows, embed), BF16),
+            pltpu.VMEM((groups, dp_n, rows, tall), BF16),
+            pltpu.SemaphoreType.DMA((copies,)),
+            pltpu.SemaphoreType.DMA((copies,)),
+        ],
+        compiler_params=pltpu.CompilerParams(
+            collective_id=0, has_side_effects=True, vmem_limit_bytes=48 * 2**20
+        ),
+    )(img_feat, txt_feat, img_weight, txt_weight, log_temp, bias)
+    whole = tiles.transpose(0, 2, 1, 3).reshape(SIDE, wide, embed).astype(F32)
+    return (whole[0], whole[1])
+
+
+def on_device(dp_n, groups, img_feat, txt_feat, img_weight, txt_weight, log_temp, bias):
+    arrays = (img_feat, txt_feat, img_weight, txt_weight, log_temp, bias)
+    rows = img_feat.shape[0]
+    wide, embed = img_weight.shape
+    depth_n = dp_n // SIDE
+    held = embed * rows * (12 * SIDE * groups + 10 * depth_n + 28 * groups)
+    held += 2 * rows * dp_n * groups * (wide + embed // depth_n) + 12 * wide * embed
+    if (
+        dp_n % SIDE or groups != 4 or rows % 16 or wide % 128
+        or embed % (128 * depth_n) or held > 40 * 2**20
+    ):
+        return by_collectives(*arrays)
+    return in_one_kernel(dp_n, groups, *arrays)
+
+
 def solution(mesh):
     placed = (
         P(("dp", "fsdp"), None),
@@ -99,7 +370,7 @@
         P(),
     )
     return jax.shard_map(
-        on_device,
+        functools.partial(on_device, mesh.shape["dp"], mesh.shape["fsdp"]),
         mesh=mesh,
         in_specs=placed,
         out_specs=(P("fsdp", None), P("fsdp", None)),

time: 427 us -> 140 us (0.33)
  the two profiles are of different devices: /device:TPU:0 before, /device:TPU:28 now
where the time goes in v1:
time: 140 us
  Pallas kernels  122 us (87%)
  local copies, waits for them, and re-layouts  14.8 us (11%)
  between operations  1.97 us (1%)
    pallas_call x1, Pallas kernels, in_one_kernel(): pl.pallas_call(functools.partial(kernel, (dp_n, groups, rows, width, embe...  122 us
    unnamed x10, local copies, waits for them, and re-layouts  8.26 us
    slice x3, local copies, waits for them, and re-layouts, in_one_kernel(): return (whole[0], whole[1])  6.59 us

profile of v1, /device:TPU:28, one launch (start us, length us, event | category | flops | bytes accessed | tf_op | source)
XLA Modules:
  0.0 139.5 jit_solution(4361716484737716343)
XLA Ops:
  1.9 0.0 copy-start
  1.9 1.3 copy-done
  3.2 0.0 copy-start.1
  3.2 1.3 copy-done.1
  4.5 0.0 copy-start.2
  4.5 0.9 copy-done.2
  5.4 0.0 copy-start.3
  5.4 0.9 copy-done.3
  6.3 122.4 %shard_map.77 = bf16[2,4,384,384]{3,2,1,0:T(8,128)(2,1)S(1)} custom-call(bf16[48,1536]{1,0:T(8,128)(2,1)S(1)} %copy-done.2, bf16[48,1536]{1,0:T(8,128)(2,1)S(1)} %copy-done.3, bf16[384,1536]{1,0:T(8,128)(2,1)S(1)} %copy-done, bf16[384,1536]{1,0:T(8,128)(2,1)S(1)} %copy-done.1, f32[1]{0:T(128)S(6)} %copy.12.log_temp, f32[1]{0:T(128)S(6)} %copy.13.bias), custom_call_target="tpu_custom_call" | custom-call | tf_op jit(solution)/shard_map/pallas_call | solution.py:315
  128.7 0.3 convert_bitcast_fusion
  129.0 2.5 %fusion = (f32[1,384,4,384]{3,1,2,0:T(8,128)}, f32[1,384,4,384]{3,1,2,0:T(8,128)}) fusion(f32[2,384,4,384]{3,1,2,0:T(8,128)S(1)} %convert_bitcast_fusion), kind=kLoop, calls=%fused_computation.1 | loop fusion | bytes 9437184 | tf_op jit(solution)/shard_map/slice | solution.py:345
  131.5 2.0 %copy.9 = f32[1,384,4,384]{1,3,2,0:T(8,128)S(1)} copy(f32[1,384,4,384]{3,1,2,0:T(8,128)} %get-tuple-element.4) | data formatting | bytes 4718592 | tf_op jit(solution)/shard_map/slice | solution.py:345
  133.6 2.0 %copy.11 = f32[384,1536]{1,0:T(8,128)} copy(f32[384,1536]{0,1:T(8,128)S(1)} %bitcast.4) | data formatting | bytes 4718592
  135.5 2.0 %copy.8 = f32[1,384,4,384]{1,3,2,0:T(8,128)S(1)} copy(f32[1,384,4,384]{3,1,2,0:T(8,128)} %get-tuple-element.5) | data formatting | bytes 4718592 | tf_op jit(solution)/shard_map/slice | solution.py:345
  137.6 2.0 %copy.10 = f32[384,1536]{1,0:T(8,128)} copy(f32[384,1536]{0,1:T(8,128)S(1)} %bitcast.5) | data formatting | bytes 4718592
Async XLA Ops:
  1.9 1.3 copy-start
  3.2 1.3 copy-start.1
  4.5 0.9 copy-start.2
  5.4 0.9 copy-start.3

commit v2 on v1

--- a/solution.py
+++ b/solution.py
@@ -103,10 +103,10 @@
 
 
 def kernel(
-    dims, img, txt, w_img, w_txt, log_temp, bias, out,
-    cols, feats, part, part16, part_in, y_keep, z_img, z_txt,
+    dims, img, txt, w_img_hbm, w_txt_hbm, log_temp, bias, out,
+    w_img, w_txt, cols, feats, part, part16, part_in, y_keep, z_img, z_txt,
     d_img, d_img16, d_img_in, d_txt, d_txt16, d_txt_in, dy, dy_all,
-    send_sem, recv_sem,
+    send_sem, recv_sem, local_sem, line_send, line_recv, over_send, over_recv,
 ):
     dp_n, groups, rows, width, embed = dims
     depth_n = dp_n // SIDE
@@ -141,6 +141,53 @@
     def lanes(start, size):
         return pl.ds(pl.multiple_of(start * size, size), size)
 
+    def line_hop(use, view, way, step):
+        place, to = depth + way * step, depth - way
+        return pltpu.make_async_remote_copy(
+            src_ref=view(place), dst_ref=view(place),
+            send_sem=line_send.at[use, (way + 1) // 2, step],
+            recv_sem=line_recv.at[use, (way + 1) // 2, step],
+            device_id=(to * SIDE + side, me_f), device_id_type=pl.DeviceIdType.MESH,
+        )
+
+    def on_line(place):
+        return (place >= 0) & (place < depth_n)
+
+    def line_step(use, view, step, then=None):
+        for way in (-1, 1):
+            place, to = depth + way * step, depth - way
+
+            if step > 0:
+                @pl.when(on_line(place))
+                def _(way=way):
+                    line_hop(use, view, way, step - 1).wait_recv()
+
+            if step < depth_n - 1:
+                @pl.when(on_line(place) & on_line(to))
+                def _(way=way):
+                    line_hop(use, view, way, step).start()
+
+            if then is not None and (step > 0 or way > 0):
+                @pl.when(on_line(place))
+                def _(way=way, place=place):
+                    then(way, step, place)
+
+    def line_sent(use, view):
+        for step in range(depth_n - 1):
+            for way in (-1, 1):
+                @pl.when(on_line(depth + way * step) & on_line(depth - way))
+                def _(way=way, step=step):
+                    line_hop(use, view, way, step).wait_send()
+
+    own_copies = [
+        pltpu.make_async_copy(img.at[:, lanes(me_f, wide)], cols.at[0, me_f], local_sem.at[0]),
+        pltpu.make_async_copy(txt.at[:, lanes(me_f, wide)], cols.at[1, me_f], local_sem.at[1]),
+        pltpu.make_async_copy(w_img_hbm, w_img, local_sem.at[2]),
+        pltpu.make_async_copy(w_txt_hbm, w_txt, local_sem.at[3]),
+    ]
+    for copy in own_copies:
+        copy.start()
+
     barrier = pltpu.get_barrier_semaphore()
     peers = [at_spot(k) for k in range(1, plane_n)]
     peers += [
@@ -157,8 +204,8 @@
             got_cols.append(
                 send(feat.at[:, lanes(to_f, wide)], cols.at[tower, me_f], me_dp, to_f)
             )
-    for tower, feat in ((1, txt), (0, img)):
-        cols[tower, me_f] = feat[:, lanes(me_f, wide)]
+    for copy in own_copies:
+        copy.wait()
 
     tile = 384 if embed % 384 == 0 else 128
     got_part = {}
@@ -181,11 +228,15 @@
             for k in range(1, groups)
         ]
 
+    def feat_pair(place):
+        return feats.at[pl.ds(place * SIDE, SIDE)]
+
+    beside = depth * SIDE + (1 - side)
     feats[me_dp] = cols[side]
-    got_feats = []
-    for k in range(1, dp_n):
-        to_dp = (me_dp + k) % dp_n
-        got_feats.append(send(cols.at[to_dp % SIDE], feats.at[me_dp], to_dp, me_f))
+    send(cols.at[1 - side], feats.at[me_dp], beside, me_f).wait_recv()
+    line_step(0, feat_pair, 0)
+    if depth_n > 2:
+        line_step(0, feat_pair, 1)
 
     def y_rows(tower):
         for copy in got_part[tower]:
@@ -206,6 +257,8 @@
     got_img = [
         send(z_img.at[spot], z_img.at[spot], *at_spot(k)) for k in range(1, plane_n)
     ]
+    for step in range(2, depth_n - 1):
+        line_step(0, feat_pair, step)
     for copy in got_txt + got_img:
         copy.wait_recv()
 
@@ -265,7 +318,8 @@
                  to_dp, me_f)
         )
     dy_all[me_f, me_dp] = dy[side, :, lanes(depth, tall)]
-    for copy in got_dy + got_feats:
+    line_step(0, feat_pair, depth_n - 1)
+    for copy in got_dy:
         copy.wait_recv()
     half = groups // 2
     across = (me_f + half) % groups
@@ -285,20 +339,28 @@
     grad = grad + grad_of(across)
     passed_on.wait_recv()
     grad = grad + grad_of((twin + half) % groups)
-    out[side, depth] = grad.astype(BF16)
-
-    beside = depth * SIDE + (1 - side)
-    along = [
-        send(out.at[side, depth], out.at[side, depth], at_depth(k) * SIDE + side, me_f)
-        for k in range(1, depth_n)
-    ]
-    over = [send(out.at[side, depth], out.at[side, depth], beside, me_f)]
-    for k in range(1, depth_n):
-        along[k - 1].wait_recv()
-        place = (depth + depth_n - k) % depth_n
-        over.append(send(out.at[side, place], out.at[side, place], beside, me_f))
-    for copy in over:
-        copy.wait_recv()
+    def out_tile(place):
+        return out.at[side, :, lanes(place, tall)]
+
+    def over_hop(way, step, place):
+        return pltpu.make_async_remote_copy(
+            src_ref=out_tile(place), dst_ref=out_tile(place),
+            send_sem=over_send.at[(way + 1) // 2, step],
+            recv_sem=over_recv.at[(way + 1) // 2, step],
+            device_id=(beside, me_f), device_id_type=pl.DeviceIdType.MESH,
+        )
+
+    out[side, :, lanes(depth, tall)] = grad.astype(BF16)
+    for step in range(depth_n):
+        line_step(1, out_tile, step, lambda *at: over_hop(*at).start())
+    for step in range(depth_n):
+        for way in (-1, 1):
+            if step > 0 or way > 0:
+                @pl.when(on_line(depth + way * step))
+                def _(way=way, step=step):
+                    over_hop(way, step, depth + way * step).wait()
+    line_sent(0, feat_pair)
+    line_sent(1, out_tile)
     for copy in sent:
         copy.wait_send()
 
@@ -308,16 +370,18 @@
     wide, embed = img_weight.shape
     depth_n, plane_n = dp_n // SIDE, SIDE * groups
     tall = embed // depth_n
-    copies = 2 * 2 * (groups - 1) + 2 * (dp_n - 1) + 3 + 2 * (depth_n - 1 + plane_n - 1)
-    copies += 2 * depth_n - 1
+    copies = 2 * 2 * (groups - 1) + dp_n - 1 + 4 + 2 * (depth_n - 1 + plane_n - 1)
+    hbm = pl.BlockSpec(memory_space=pltpu.HBM)
     vmem = pl.BlockSpec(memory_space=pltpu.VMEM)
     smem = pl.BlockSpec(memory_space=pltpu.SMEM)
     tiles = pl.pallas_call(
         functools.partial(kernel, (dp_n, groups, rows, width, embed)),
-        out_shape=jax.ShapeDtypeStruct((SIDE, depth_n, wide, tall), BF16),
-        in_specs=[vmem] * 4 + [smem] * 2,
+        out_shape=jax.ShapeDtypeStruct((SIDE, wide, embed), BF16),
+        in_specs=[hbm] * 4 + [smem] * 2,
         out_specs=vmem,
         scratch_shapes=[
+            pltpu.VMEM((wide, embed), BF16),
+            pltpu.VMEM((wide, embed), BF16),
             pltpu.VMEM((2, groups, rows, wide), BF16),
             pltpu.VMEM((dp_n, groups, rows, wide), BF16),
             pltpu.VMEM((2, groups, rows, embed), F32),
@@ -336,13 +400,17 @@
             pltpu.VMEM((groups, dp_n, rows, tall), BF16),
             pltpu.SemaphoreType.DMA((copies,)),
             pltpu.SemaphoreType.DMA((copies,)),
+            pltpu.SemaphoreType.DMA((4,)),
+            pltpu.SemaphoreType.DMA((2, 2, depth_n)),
+            pltpu.SemaphoreType.DMA((2, 2, depth_n)),
+            pltpu.SemaphoreType.DMA((2, depth_n)),
+            pltpu.SemaphoreType.DMA((2, depth_n)),
         ],
         compiler_params=pltpu.CompilerParams(
             collective_id=0, has_side_effects=True, vmem_limit_bytes=48 * 2**20
         ),
     )(img_feat, txt_feat, img_weight, txt_weight, log_temp, bias)
-    whole = tiles.transpose(0, 2, 1, 3).reshape(SIDE, wide, embed).astype(F32)
-    return (whole[0], whole[1])
+    return (tiles[0].astype(F32), tiles[1].astype(F32))
 
 
 def on_device(dp_n, groups, img_feat, txt_feat, img_weight, txt_weight, log_temp, bias):

time: 140 us -> 122 us (0.87)
  the two profiles are of different devices: /device:TPU:28 before, /device:TPU:0 now
where the time goes in v2:
time: 122 us
  Pallas kernels  113 us (93%)
  local copies, waits for them, and re-layouts  4.35 us (4%)
  other arithmetic  2.83 us (2%)
  between operations  1.94 us (2%)
    pallas_call x1, Pallas kernels, in_one_kernel(): pl.pallas_call(functools.partial(kernel, (dp_n, groups, rows, width, embe...  113 us
    unnamed x8, local copies, waits for them, and re-layouts  4.35 us
    convert_element_type x1, other arithmetic, in_one_kernel(): return (tiles[0].astype(F32), tiles[1].astype(F32))  2.83 us

profile of v2, /device:TPU:0, one launch (start us, length us, event | category | flops | bytes accessed | tf_op | source)
XLA Modules:
  0.0 121.9 jit_solution(826652849059763976)
XLA Ops:
  1.9 0.0 copy-start
  1.9 1.3 %copy-done = bf16[384,1536]{1,0:T(8,128)(2,1)S(1)} copy-done((bf16[384,1536]{1,0:T(8,128)(2,1)S(1)}, bf16[384,1536]{1,0:T(8,128)(2,1)}, u32[]{:S(2)}) %copy-start) | copy-done | bytes 1179672
  3.2 0.0 copy-start.1
  3.2 1.3 %copy-done.1 = bf16[384,1536]{1,0:T(8,128)(2,1)S(1)} copy-done((bf16[384,1536]{1,0:T(8,128)(2,1)S(1)}, bf16[384,1536]{1,0:T(8,128)(2,1)}, u32[]{:S(2)}) %copy-start.1) | copy-done | bytes 1179672
  4.5 0.0 copy-start.2
  4.5 0.9 copy-done.2
  5.4 0.0 copy-start.3
  5.4 0.9 copy-done.3
  6.3 112.8 %shard_map.77 = bf16[2,384,1536]{2,1,0:T(8,128)(2,1)S(1)} custom-call(bf16[48,1536]{1,0:T(8,128)(2,1)S(1)} %copy-done.2, bf16[48,1536]{1,0:T(8,128)(2,1)S(1)} %copy-done.3, bf16[384,1536]{1,0:T(8,128)(2,1)S(1)} %copy-done, bf16[384,1536]{1,0:T(8,128)(2,1)S(1)} %copy-done.1, f32[1]{0:T(128)S(6)} %copy.8.log_temp, f32[1]{0:T(128)S(6)} %copy.9.bias), custom_call_target="tpu_custom_call" | custom-call | tf_op jit(solution)/shard_map/pallas_call | solution.py:377
  119.1 2.8 %bitcast_convert_fusion = (f32[384,1536]{1,0:T(8,128)}, f32[384,1536]{1,0:T(8,128)}) fusion(bf16[2,384,1536]{2,1,0:T(8,128)(2,1)S(1)} %shard_map.77), kind=kLoop, calls=%fused_computation | loop fusion | flops 1179648 | bytes 7077888 | tf_op jit(solution)/shard_map/convert_element_type | solution.py:413
Async XLA Ops:
  1.9 1.3 %copy-start = (bf16[384,1536]{1,0:T(8,128)(2,1)S(1)}, bf16[384,1536]{1,0:T(8,128)(2,1)}, u32[]{:S(2)}) copy-start(bf16[384,1536]{1,0:T(8,128)(2,1)} %w_img_hbm.1) | copy-start | bytes 3538948
  3.2 1.3 %copy-start.1 = (bf16[384,1536]{1,0:T(8,128)(2,1)S(1)}, bf16[384,1536]{1,0:T(8,128)(2,1)}, u32[]{:S(2)}) copy-start(bf16[384,1536]{1,0:T(8,128)(2,1)} %w_txt_hbm.1) | copy-start | bytes 3538948
  4.5 0.9 copy-start.2
  5.4 0.9 copy-start.3

commit v3 on v2

--- a/solution.py
+++ b/solution.py
@@ -96,6 +96,7 @@
 BF16 = jnp.bfloat16
 F32 = jnp.float32
 SIDE = 2
+CHUNKS = 3
 
 
 def dot(a, b, a_dim, b_dim):
@@ -104,7 +105,7 @@
 
 def kernel(
     dims, img, txt, w_img_hbm, w_txt_hbm, log_temp, bias, out,
-    w_img, w_txt, cols, feats, part, part16, part_in, y_keep, z_img, z_txt,
+    w_img, w_txt, cols, feats, part, pre_in, pre16, twin_in, part_in, y_keep, z_img, z_txt,
     d_img, d_img16, d_img_in, d_txt, d_txt16, d_txt_in, dy, dy_all,
     send_sem, recv_sem, local_sem, line_send, line_recv, over_send, over_recv,
 ):
@@ -207,43 +208,54 @@
     for copy in own_copies:
         copy.wait()
 
+    for copy in got_cols:
+        copy.wait_recv()
+
+    def feat_pair(place):
+        return feats.at[pl.ds(place * SIDE, SIDE)]
+
+    beside = depth * SIDE + (1 - side)
+    feat_beside = send(cols.at[1 - side], feats.at[me_dp], beside, me_f)
+
+    half = groups // 2
+    core = me_f % half
+    across = (me_f + half) % groups
+    twin = me_f + 1 - 2 * core
+    away = across - core
     tile = 384 if embed % 384 == 0 else 128
-    got_part = {}
+    got_pre, got_twin, got_part = {}, {}, {}
     for tower, weight in ((1, w_txt), (0, w_img)):
-        for k in range(1, groups):
-            got_cols.pop(0).wait_recv()
 
         def y_tile(j, carry, tower=tower, weight=weight):
             where = lanes(j, tile)
             term = dot(cols[tower].reshape(groups * rows, wide), weight[:, where], 1, 0)
-            term = term.reshape(groups, rows, tile)
-            part[tower, :, :, where] = term
-            part16[tower, :, :, where] = term.astype(BF16)
+            part[tower, :, :, where] = term.reshape(groups, rows, tile)
             return carry
 
         lax.fori_loop(0, embed // tile, y_tile, 0)
+        got_pre[tower] = send(
+            part.at[tower, pl.ds(away, half), :, lanes(1 - core, embed // half)],
+            pre_in.at[tower], me_dp, twin,
+        )
+        got_twin[tower] = send(part.at[tower, twin], twin_in.at[tower], me_dp, twin)
+    for tower in (1, 0):
+        got_pre[tower].wait_recv()
+        mine = part[tower, pl.ds(away, half), :, lanes(core, embed // half)]
+        pre16[tower] = (mine + pre_in[tower]).astype(BF16)
         got_part[tower] = [
-            send(part16.at[tower, (me_f + k) % groups], part_in.at[tower, k - 1],
-                 me_dp, (me_f + k) % groups)
-            for k in range(1, groups)
+            send(pre16.at[tower, n], part_in.at[tower, :, lanes(core, embed // half)],
+                 me_dp, away + n)
+            for n in ((core + k) % half for k in range(half))
         ]
-
-    def feat_pair(place):
-        return feats.at[pl.ds(place * SIDE, SIDE)]
-
-    beside = depth * SIDE + (1 - side)
     feats[me_dp] = cols[side]
-    send(cols.at[1 - side], feats.at[me_dp], beside, me_f).wait_recv()
+    feat_beside.wait_recv()
     line_step(0, feat_pair, 0)
-    if depth_n > 2:
-        line_step(0, feat_pair, 1)
 
     def y_rows(tower):
+        got_twin[tower].wait_recv()
         for copy in got_part[tower]:
             copy.wait_recv()
-        total = part[tower, me_f]
-        for k in range(1, groups):
-            total = total + part_in[tower, k - 1].astype(F32)
+        total = part[tower, me_f] + twin_in[tower] + part_in[tower].astype(F32)
         y_keep[tower] = total
         norm_factor, _ = factor(total)
         return (total * norm_factor).astype(BF16)
@@ -257,10 +269,12 @@
     got_img = [
         send(z_img.at[spot], z_img.at[spot], *at_spot(k)) for k in range(1, plane_n)
     ]
+    if depth_n > 2:
+        line_step(0, feat_pair, 1)
+    for copy in got_txt + got_img:
+        copy.wait_recv()
     for step in range(2, depth_n - 1):
         line_step(0, feat_pair, step)
-    for copy in got_txt + got_img:
-        copy.wait_recv()
 
     n_img, n_txt = plane_n * rows, depth_n * rows
     scale = jnp.exp(jnp.full((1, n_txt), log_temp[0], F32))
@@ -321,9 +335,6 @@
     line_step(0, feat_pair, depth_n - 1)
     for copy in got_dy:
         copy.wait_recv()
-    half = groups // 2
-    across = (me_f + half) % groups
-    twin = me_f + 1 - 2 * (me_f % 2)
     from_across = send(dy_all.at[me_f], dy_all.at[me_f], me_dp, across)
     from_twin = send(dy_all.at[me_f], dy_all.at[me_f], me_dp, twin)
 
@@ -339,28 +350,33 @@
     grad = grad + grad_of(across)
     passed_on.wait_recv()
     grad = grad + grad_of((twin + half) % groups)
-    def out_tile(place):
-        return out.at[side, :, lanes(place, tall)]
-
-    def over_hop(way, step, place):
+    def out_tile(chunk):
+        deep = wide // CHUNKS
+        return lambda place: out.at[side, pl.ds(chunk * deep, deep), lanes(place, tall)]
+
+    def over_hop(chunk, way, step, place):
         return pltpu.make_async_remote_copy(
-            src_ref=out_tile(place), dst_ref=out_tile(place),
-            send_sem=over_send.at[(way + 1) // 2, step],
-            recv_sem=over_recv.at[(way + 1) // 2, step],
+            src_ref=out_tile(chunk)(place), dst_ref=out_tile(chunk)(place),
+            send_sem=over_send.at[chunk, (way + 1) // 2, step],
+            recv_sem=over_recv.at[chunk, (way + 1) // 2, step],
             device_id=(beside, me_f), device_id_type=pl.DeviceIdType.MESH,
         )
 
     out[side, :, lanes(depth, tall)] = grad.astype(BF16)
     for step in range(depth_n):
-        line_step(1, out_tile, step, lambda *at: over_hop(*at).start())
+        for chunk in range(CHUNKS):
+            line_step(1 + chunk, out_tile(chunk), step,
+                      lambda *at, chunk=chunk: over_hop(chunk, *at).start())
     for step in range(depth_n):
         for way in (-1, 1):
             if step > 0 or way > 0:
                 @pl.when(on_line(depth + way * step))
                 def _(way=way, step=step):
-                    over_hop(way, step, depth + way * step).wait()
+                    for chunk in range(CHUNKS):
+                        over_hop(chunk, way, step, depth + way * step).wait()
     line_sent(0, feat_pair)
-    line_sent(1, out_tile)
+    for chunk in range(CHUNKS):
+        line_sent(1 + chunk, out_tile(chunk))
     for copy in sent:
         copy.wait_send()
 
@@ -370,7 +386,7 @@
     wide, embed = img_weight.shape
     depth_n, plane_n = dp_n // SIDE, SIDE * groups
     tall = embed // depth_n
-    copies = 2 * 2 * (groups - 1) + dp_n - 1 + 4 + 2 * (depth_n - 1 + plane_n - 1)
+    copies = 2 * (groups - 1) + 8 + dp_n - 1 + 4 + 2 * (depth_n - 1 + plane_n - 1)
     hbm = pl.BlockSpec(memory_space=pltpu.HBM)
     vmem = pl.BlockSpec(memory_space=pltpu.VMEM)
     smem = pl.BlockSpec(memory_space=pltpu.SMEM)
@@ -385,8 +401,10 @@
             pltpu.VMEM((2, groups, rows, wide), BF16),
             pltpu.VMEM((dp_n, groups, rows, wide), BF16),
             pltpu.VMEM((2, groups, rows, embed), F32),
-            pltpu.VMEM((2, groups, rows, embed), BF16),
-            pltpu.VMEM((2, groups - 1, rows, embed), BF16),
+            pltpu.VMEM((2, groups // 2, rows, embed // 2), F32),
+            pltpu.VMEM((2, groups // 2, rows, embed // 2), BF16),
+            pltpu.VMEM((2, rows, embed), F32),
+            pltpu.VMEM((2, rows, embed), BF16),
             pltpu.VMEM((2, rows, embed), F32),
             pltpu.VMEM((plane_n, rows, embed), BF16),
             pltpu.VMEM((depth_n, rows, embed), BF16),
@@ -401,13 +419,13 @@
             pltpu.SemaphoreType.DMA((copies,)),
             pltpu.SemaphoreType.DMA((copies,)),
             pltpu.SemaphoreType.DMA((4,)),
-            pltpu.SemaphoreType.DMA((2, 2, depth_n)),
-            pltpu.SemaphoreType.DMA((2, 2, depth_n)),
-            pltpu.SemaphoreType.DMA((2, depth_n)),
-            pltpu.SemaphoreType.DMA((2, depth_n)),
+            pltpu.SemaphoreType.DMA((1 + CHUNKS, 2, depth_n)),
+            pltpu.SemaphoreType.DMA((1 + CHUNKS, 2, depth_n)),
+            pltpu.SemaphoreType.DMA((CHUNKS, 2, depth_n)),
+            pltpu.SemaphoreType.DMA((CHUNKS, 2, depth_n)),
         ],
         compiler_params=pltpu.CompilerParams(
-            collective_id=0, has_side_effects=True, vmem_limit_bytes=48 * 2**20
+            collective_id=0, has_side_effects=True, vmem_limit_bytes=61 * 2**20
         ),
     )(img_feat, txt_feat, img_weight, txt_weight, log_temp, bias)
     return (tiles[0].astype(F32), tiles[1].astype(F32))
@@ -421,7 +439,8 @@
     held = embed * rows * (12 * SIDE * groups + 10 * depth_n + 28 * groups)
     held += 2 * rows * dp_n * groups * (wide + embed // depth_n) + 12 * wide * embed
     if (
-        dp_n % SIDE or groups != 4 or rows % 16 or wide % 128
+        dp_n % SIDE or groups != 4 or rows % 16 or wide % 128 or wide % (16 * CHUNKS)
+        or embed % 256
         or embed % (128 * depth_n) or held > 40 * 2**20
     ):
         return by_collectives(*arrays)

time: 122 us -> 112 us (0.918)
  Pallas kernels: 113 us -> 105 us
  local copies, waits for them, and re-layouts: 4.35 us -> 0 us
  other arithmetic: 2.83 us -> 4.46 us
    pallas_call x1, Pallas kernels: 113 us -> 105 us  [in_one_kernel(): pl.pallas_call(functools.partial(kernel, (dp_n, groups, rows, width, embe...]
    unnamed x8 -> x0, local copies, waits for them, and re-layouts: 4.35 us -> none
    convert_element_type x1, other arithmetic: 2.83 us -> 4.46 us  [in_one_kernel(): return (tiles[0].astype(F32), tiles[1].astype(F32))]
where the time goes in v3:
time: 112 us
  Pallas kernels  105 us (94%)
  other arithmetic  4.46 us (4%)
  between operations  1.93 us (2%)
    pallas_call x1, Pallas kernels, in_one_kernel(): pl.pallas_call(functools.partial(kernel, (dp_n, groups, rows, width, embe...  105 us
    convert_element_type x1, other arithmetic, in_one_kernel(): return (tiles[0].astype(F32), tiles[1].astype(F32))  4.46 us

profile of v3, /device:TPU:0, one launch (start us, length us, event | category | flops | bytes accessed | tf_op | source)
XLA Modules:
  0.0 111.6 jit_solution(13747250895005391771)
XLA Ops:
  1.9 105.2 %shard_map.77 = bf16[2,384,1536]{2,1,0:T(8,128)(2,1)} custom-call(bf16[48,1536]{1,0:T(8,128)(2,1)} %img.1, bf16[48,1536]{1,0:T(8,128)(2,1)} %txt.1, bf16[384,1536]{1,0:T(8,128)(2,1)} %w_img_hbm.1, bf16[384,1536]{1,0:T(8,128)(2,1)} %w_txt_hbm.1, f32[1]{0:T(128)S(6)} %copy.8.log_temp, f32[1]{0:T(128)S(6)} %copy.9.bias), custom_call_target="tpu_custom_call" | custom-call | tf_op jit(solution)/shard_map/pallas_call | solution.py:393
  107.1 4.5 %bitcast_convert_fusion = (f32[384,1536]{1,0:T(8,128)}, f32[384,1536]{1,0:T(8,128)}) fusion(bf16[2,384,1536]{2,1,0:T(8,128)(2,1)} %shard_map.77), kind=kLoop, calls=%fused_computation | loop fusion | flops 1179648 | bytes 7077888 | tf_op jit(solution)/shard_map/convert_element_type | solution.py:431

commit v4 on v3

--- a/solution.py
+++ b/solution.py
@@ -211,11 +211,16 @@
     for copy in got_cols:
         copy.wait_recv()
 
-    def feat_pair(place):
-        return feats.at[pl.ds(place * SIDE, SIDE)]
+    def feat_own(place):
+        return feats.at[place * SIDE + side]
+
+    def feat_other(place):
+        return feats.at[place * SIDE + 1 - side]
 
     beside = depth * SIDE + (1 - side)
     feat_beside = send(cols.at[1 - side], feats.at[me_dp], beside, me_f)
+    feats[me_dp] = cols[side]
+    line_step(0, feat_own, 0)
 
     half = groups // 2
     core = me_f % half
@@ -238,6 +243,8 @@
             pre_in.at[tower], me_dp, twin,
         )
         got_twin[tower] = send(part.at[tower, twin], twin_in.at[tower], me_dp, twin)
+    feat_beside.wait_recv()
+    line_step(1, feat_other, 0)
     for tower in (1, 0):
         got_pre[tower].wait_recv()
         mine = part[tower, pl.ds(away, half), :, lanes(core, embed // half)]
@@ -247,10 +254,8 @@
                  me_dp, away + n)
             for n in ((core + k) % half for k in range(half))
         ]
-    feats[me_dp] = cols[side]
-    feat_beside.wait_recv()
-    line_step(0, feat_pair, 0)
-
+    if depth_n > 2:
+        line_step(0, feat_own, 1)
     def y_rows(tower):
         got_twin[tower].wait_recv()
         for copy in got_part[tower]:
@@ -270,11 +275,12 @@
         send(z_img.at[spot], z_img.at[spot], *at_spot(k)) for k in range(1, plane_n)
     ]
     if depth_n > 2:
-        line_step(0, feat_pair, 1)
+        line_step(1, feat_other, 1)
     for copy in got_txt + got_img:
         copy.wait_recv()
     for step in range(2, depth_n - 1):
-        line_step(0, feat_pair, step)
+        line_step(0, feat_own, step)
+        line_step(1, feat_other, step)
 
     n_img, n_txt = plane_n * rows, depth_n * rows
     scale = jnp.exp(jnp.full((1, n_txt), log_temp[0], F32))
@@ -332,7 +338,8 @@
                  to_dp, me_f)
         )
     dy_all[me_f, me_dp] = dy[side, :, lanes(depth, tall)]
-    line_step(0, feat_pair, depth_n - 1)
+    line_step(0, feat_own, depth_n - 1)
+    line_step(1, feat_other, depth_n - 1)
     for copy in got_dy:
         copy.wait_recv()
     from_across = send(dy_all.at[me_f], dy_all.at[me_f], me_dp, across)
@@ -365,7 +372,7 @@
     out[side, :, lanes(depth, tall)] = grad.astype(BF16)
     for step in range(depth_n):
         for chunk in range(CHUNKS):
-            line_step(1 + chunk, out_tile(chunk), step,
+            line_step(2 + chunk, out_tile(chunk), step,
                       lambda *at, chunk=chunk: over_hop(chunk, *at).start())
     for step in range(depth_n):
         for way in (-1, 1):
@@ -374,9 +381,10 @@
                 def _(way=way, step=step):
                     for chunk in range(CHUNKS):
                         over_hop(chunk, way, step, depth + way * step).wait()
-    line_sent(0, feat_pair)
+    line_sent(0, feat_own)
+    line_sent(1, feat_other)
     for chunk in range(CHUNKS):
-        line_sent(1 + chunk, out_tile(chunk))
+        line_sent(2 + chunk, out_tile(chunk))
     for copy in sent:
         copy.wait_send()
 
@@ -419,8 +427,8 @@
             pltpu.SemaphoreType.DMA((copies,)),
             pltpu.SemaphoreType.DMA((copies,)),
             pltpu.SemaphoreType.DMA((4,)),
-            pltpu.SemaphoreType.DMA((1 + CHUNKS, 2, depth_n)),
-            pltpu.SemaphoreType.DMA((1 + CHUNKS, 2, depth_n)),
+            pltpu.SemaphoreType.DMA((2 + CHUNKS, 2, depth_n)),
+            pltpu.SemaphoreType.DMA((2 + CHUNKS, 2, depth_n)),
             pltpu.SemaphoreType.DMA((CHUNKS, 2, depth_n)),
             pltpu.SemaphoreType.DMA((CHUNKS, 2, depth_n)),
         ],

time: 112 us -> 110 us (0.982)
  Pallas kernels: 105 us -> 103 us
    pallas_call x1, Pallas kernels: 105 us -> 103 us  [in_one_kernel(): pl.pallas_call(functools.partial(kernel, (dp_n, groups, rows, width, embe...]
where the time goes in v4:
time: 110 us; the launch traced here: 109 us
  Pallas kernels  103 us (94%)
  other arithmetic  4.46 us (4%)
  between operations  1.93 us (2%)
    pallas_call x1, Pallas kernels, in_one_kernel(): pl.pallas_call(functools.partial(kernel, (dp_n, groups, rows, width, embe...  103 us
    convert_element_type x1, other arithmetic, in_one_kernel(): return (tiles[0].astype(F32), tiles[1].astype(F32))  4.46 us

profile of v4, /device:TPU:0, one launch (start us, length us, event | category | flops | bytes accessed | tf_op | source)
XLA Modules:
  0.0 109.5 jit_solution(1014800575930278474)
XLA Ops:
  1.9 103.1 %shard_map.77 = bf16[2,384,1536]{2,1,0:T(8,128)(2,1)} custom-call(bf16[48,1536]{1,0:T(8,128)(2,1)} %img.1, bf16[48,1536]{1,0:T(8,128)(2,1)} %txt.1, bf16[384,1536]{1,0:T(8,128)(2,1)} %w_img_hbm.1, bf16[384,1536]{1,0:T(8,128)(2,1)} %w_txt_hbm.1, f32[1]{0:T(128)S(6)} %copy.8.log_temp, f32[1]{0:T(128)S(6)} %copy.9.bias), custom_call_target="tpu_custom_call" | custom-call | tf_op jit(solution)/shard_map/pallas_call | solution.py:401
  105.0 4.5 %bitcast_convert_fusion = (f32[384,1536]{1,0:T(8,128)}, f32[384,1536]{1,0:T(8,128)}) fusion(bf16[2,384,1536]{2,1,0:T(8,128)(2,1)} %shard_map.77), kind=kLoop, calls=%fused_computation | loop fusion | flops 1179648 | bytes 7077888 | tf_op jit(solution)/shard_map/convert_element_type | solution.py:439
